TPU v7x, 512 devices: a whole 4x8x8 slice. The times are simulated.
512 devices in a mesh: row: 32 (over y_lo, z, core), col: 16 (over x, y_hi).
Axes of the slice: x: 4, y: 8 (y_hi: 4, y_lo: 2; y = y_hi * 2 + y_lo), z: 8, core: 2. Of those that a mesh axis runs over, the one named last changes fastest.
Arguments:
- inputs: bfloat16 [512, 12288], P('col', 'row'), may hold values from -6 to 6
- out_grad: bfloat16 [512, 12288], P('col', 'row'), may hold values from -5 to 5
- w_in: bfloat16 [12288, 24576], P('row', 'col'), may hold values from -0.0546875 to 0.0546875
- w_out: bfloat16 [24576, 12288], P('col', 'row'), may hold values from -0.0390625 to 0.0390625
Outputs:
- grad_inputs: bfloat16 [512, 12288], P('col', 'row')
- grad_w_in: bfloat16 [12288, 24576], P('row', 'col')
- grad_w_out: bfloat16 [24576, 12288], P('col', 'row')
All inputs are finite; a program needn't handle non-finite values.
Results may differ from a plain program's by a relative error of at most 0.0049.
Values may be sent and summed in bfloat16 or wider, within the bound.
A program may use at most 64 MiB of HBM per device.

v0:
```python
import jax
import jax.numpy as jnp
from jax import lax
from jax.sharding import PartitionSpec as P

slope_const = 0.7978845608028654
cubic_coef = 0.044715


def gelu_value(v):
    inner = slope_const * (v + cubic_coef * v * v * v)
    return 0.5 * v * (1.0 + jnp.tanh(inner))


def gelu_slope(v):
    inner = slope_const * (v + cubic_coef * v * v * v)
    tanh_val = jnp.tanh(inner)
    deriv = slope_const * (1.0 + 3.0 * cubic_coef * v * v)
    return 0.5 * (1.0 + tanh_val) + 0.5 * v * (1.0 - tanh_val * tanh_val) * deriv


def right_trans(left, right):
    return lax.dot_general(
        left, right, (((1,), (1,)), ((), ())), preferred_element_type=jnp.float32
    )


def left_trans(left, right):
    return lax.dot_general(
        left, right, (((0,), (0,)), ((), ())), preferred_element_type=jnp.float32
    )


def activate(preact, upstream):
    activation = gelu_value(preact).astype(jnp.bfloat16)
    hidden_grad = (upstream * gelu_slope(preact)).astype(jnp.bfloat16)
    return (activation, hidden_grad)


def body(inputs, out_grad, w_in, w_out):
    tok_panel, grad_panel = (
        lax.all_gather(inputs, "col", axis=0, tiled=True),
        lax.all_gather(out_grad, "col", axis=0, tiled=True),
    )
    preact_part = jnp.dot(tok_panel, w_in, preferred_element_type=jnp.float32)
    upstream_part = right_trans(grad_panel, w_out)
    preact, upstream = lax.psum((preact_part, upstream_part), "row")
    activation, hidden_grad = activate(preact, upstream)
    grad_w_in = left_trans(tok_panel, hidden_grad).astype(jnp.bfloat16)
    grad_w_out = left_trans(activation, grad_panel).astype(jnp.bfloat16)
    grad_inputs = lax.psum_scatter(
        right_trans(hidden_grad, w_in), "col", scatter_dimension=0, tiled=True
    ).astype(jnp.bfloat16)
    return (grad_inputs, grad_w_in, grad_w_out)


def solution(mesh):
    return jax.shard_map(
        body,
        mesh=mesh,
        in_specs=(P("col", "row"), P("col", "row"), P("row", "col"), P("col", "row")),
        out_specs=(P("col", "row"), P("row", "col"), P("col", "row")),
        check_vma=False,
    )
```

profile of v0, /device:TPU:1, one launch (start us, length us, event | category | flops | bytes accessed | tf_op | source)
XLA Modules:
  0.0 452.4 jit_solution(8699713935752455943)
XLA Ops:
  7.2 0.0 copy-start
  7.2 0.0 all-reduce.3.cloned.1.call-start
  7.2 41.0 %all_gather.7 = bf16[512,384]{1,0:T(8,128)(2,1)S(1)} all-gather(bf16[32,384]{1,0:T(8,128)(2,1)} %param.4), channel_id=1, replica_groups=mesh['row'=32,'col'=16] {'col'}, dimensions={0}, use_global_device_ids=true | all-gather | bytes 417792 | tf_op jit(solution)/shard_map/all_gather | solution.py:42
  48.2 34.4 %all_gather.6 = bf16[512,384]{1,0:T(8,128)(2,1)S(1)} all-gather(bf16[32,384]{1,0:T(8,128)(2,1)} %param.5), channel_id=1, replica_groups=mesh['row'=32,'col'=16] {'col'}, dimensions={0}, use_global_device_ids=true | all-gather | bytes 417792 | tf_op jit(solution)/shard_map/all_gather | solution.py:43
  82.6 4.0 fusion.13
  86.6 0.0 copy-done
  86.6 2.6 fusion.14
  89.2 0.0 all-reduce.3.cloned.1.call-update
  89.2 0.0 reduce-scatter.2.cloned.1.call-start
  89.3 260.9 %all-reduce.3.cloned.1.call-done = (f32[512,1536]{1,0:T(8,128)}, f32[512,1536]{1,0:T(8,128)}) async-done(((f32[512,1536]{1,0:T(8,128)}, f32[512,1536]{1,0:T(8,128)}), (f32[512,1536]{1,0:T(8,128)}, f32[512,1536]{1,0:T(8,128)})) %all-reduce.3.cloned.1.call-update) | async-done | bytes 6291472 | tf_op jit(solution)/shard_map/psum | solution.py:47
  350.2 3.9 fusion.7
  354.1 1.9 fusion.15
  356.0 0.0 reduce-scatter.2.cloned.1.call-update
  356.0 2.0 fusion.8
  358.1 2.4 copy.7
  360.4 4.3 convolution_convert_fusion
  364.7 79.4 %reduce-scatter.2.cloned.1.call-done = f32[32,384]{1,0:T(8,128)} async-done(((f32[512,384]{1,0:T(8,128)}), f32[32,384]{1,0:T(8,128)}) %reduce-scatter.2.cloned.1.call-update) | async-done | bytes 49168 | tf_op jit(solution)/shard_map/reduce_scatter | solution.py:51
  444.1 1.4 convert_element_type.19
Async XLA Ops:
  7.2 79.4 %copy-start = (bf16[384,1536]{1,0:T(8,128)(2,1)S(1)}, bf16[384,1536]{1,0:T(8,128)(2,1)}, u32[]{:S(2)}) copy-start(bf16[384,1536]{1,0:T(8,128)(2,1)} %param.6) | copy-start | bytes 3538948
  7.2 343.0 %all-reduce.3.cloned.1.call-start = ((), (), s32[]{:S(2)}) async-start(), calls=%async_computation.2 | async-start | bytes 12582912 | tf_op jit(solution)/shard_map/psum | solution.py:47
  89.2 354.9 %reduce-scatter.2.cloned.1.call-start = ((), (), s32[]{:S(2)}) async-start(), calls=%async_computation.1 | async-start | bytes 835584 | tf_op jit(solution)/shard_map/reduce_scatter | solution.py:51
Sparse Core Ops, SparseCore 0:
  89.3 260.8 all-reduce.2
  356.1 87.9 reduce-scatter.1
where the time goes:
time: 453 us; the launch traced here: 452 us
  waiting for transfers between devices  340 us (75%)
  blocking collectives  75.4 us (17%)
  matrix products  14.8 us (3%)
  between operations  14.1 us (3%)
  other arithmetic  5.31 us (1%)
    psum x1, waiting for transfers between devices, body(): preact, upstream = lax.psum((preact_part, upstream_part), 'row')  261 us
    reduce_scatter x1, waiting for transfers between devices, body(): lax.psum_scatter(right_trans(hidden_grad, w_in), 'col', scatter_dimension...  79.4 us
    all_gather x1, blocking collectives, body(): lax.all_gather(inputs, 'col', axis=0, tiled=True)  41 us
    all_gather x1, blocking collectives, body(): lax.all_gather(out_grad, 'col', axis=0, tiled=True)  34.4 us
  transfers between devices with their start and end apart: 2, of which 2 were waited for; matrix products, arithmetic and copies ran while one was open for 2% of the time, Pallas kernels for 0%

commit v1 on v0

v1 whole, which is shorter than its diff:
```python
import functools

import jax
import jax.numpy as jnp
from jax import lax
from jax.experimental import pallas as pl
from jax.experimental.pallas import tpu as pltpu
from jax.sharding import PartitionSpec as P

MESH = pl.DeviceIdType.MESH
BF16 = jnp.bfloat16
F32 = jnp.float32

slope_const = 0.7978845608028654
cubic_coef = 0.044715

NX, NYH, NYL, NZ = 4, 4, 2, 8
TOKENS = 512
BLOCK = TOKENS // NX
PIECE = BLOCK // NYH
CHUNK = BLOCK // NZ
WIDTH = 384
HIDDEN = 1536
HALF = HIDDEN // 2


def nt(left, right):
    return lax.dot_general(
        left, right, (((1,), (1,)), ((), ())), preferred_element_type=F32
    )


def tn(left, right):
    return lax.dot_general(
        left, right, (((0,), (0,)), ((), ())), preferred_element_type=F32
    )


def activate(preact, upstream):
    square = preact * preact
    inner = slope_const * (preact + cubic_coef * square * preact)
    tanh_val = jnp.tanh(inner)
    deriv = slope_const * (1.0 + 3.0 * cubic_coef * square)
    value = 0.5 * preact * (1.0 + tanh_val)
    slope = 0.5 * (1.0 + tanh_val) + 0.5 * preact * (1.0 - tanh_val * tanh_val) * deriv
    return value.astype(BF16), (upstream * slope).astype(BF16)


def kernel(
    inputs, out_grad, w_in, w_out,
    grad_inputs, grad_w_in, grad_w_out,
    panel, wi, wo, w_full, part, rs_out, rs_in, y_out, y_in, ah,
    x_out, x_in, gx, gy_out, gy_in, gi_stage, gwi_stage, gwo_stage,
    local_sem, core_s, core_r, wx_s, wx_r, ys_s, ys_r, xs_s, xs_r, xf_s, xf_r,
    rs_s, rs_r, ye_s, ye_r, ag_s, ag_r, cf_s, cf_r, gx_s, gx_r, gy_s, gy_r,
):
    row, col = lax.axis_index("row"), lax.axis_index("col")
    y_lo, z, core = row // 16, (row // 2) % 8, row % 2
    x, y_hi = col // 4, col % 4
    other = 1 - core

    def device(y_lo=y_lo, z=z, core=core, x=x, y_hi=y_hi):
        return ((y_lo * NZ + z) * 2 + core, x * NYH + y_hi)

    twin = device(core=other)
    partner = device(y_lo=1 - y_lo)
    z_next = (device(z=(z + 1) % NZ), device(z=(z + NZ - 1) % NZ))
    x_next = (device(x=(x + 1) % NX), device(x=(x + NX - 1) % NX))
    x_far = device(x=(x + 2) % NX)
    y_peer = [device(y_hi=(y_hi + j + 1) % NYH) for j in range(3)]

    def remote(src, dst, send, recv, to):
        return pltpu.make_async_remote_copy(
            src_ref=src, dst_ref=dst, send_sem=send, recv_sem=recv,
            device_id=to, device_id_type=MESH,
        )

    def at16(start, size):
        return pl.ds(pl.multiple_of(start, 16), size)

    my_rows = at16(x * BLOCK + y_hi * PIECE, PIECE)
    half_cols = pl.ds(pl.multiple_of(core * HALF, 128), HALF)
    other_cols = pl.ds(pl.multiple_of(other * HALF, 128), HALF)
    own = [
        pltpu.make_async_copy(inputs, panel.at[0, my_rows, 0:WIDTH], local_sem.at[0]),
        pltpu.make_async_copy(out_grad, panel.at[1, my_rows, 0:WIDTH], local_sem.at[1]),
        pltpu.make_async_copy(w_in.at[:, half_cols], wi.at[0:WIDTH, :], local_sem.at[2]),
        pltpu.make_async_copy(w_out.at[half_cols, :], wo.at[:, 0:WIDTH], local_sem.at[3]),
        pltpu.make_async_copy(w_in, w_full, local_sem.at[4]),
    ]
    for copy in own:
        copy.start()

    barrier = pltpu.get_barrier_semaphore()
    greeted = [twin, partner, *z_next, *x_next, x_far, *y_peer]
    for peer in greeted:
        pl.semaphore_signal(barrier, inc=1, device_id=peer, device_id_type=MESH)
    pl.semaphore_wait(barrier, len(greeted))

    own[0].wait()
    own[1].wait()

    def piece_rows(block, j):
        return at16(block * BLOCK + ((y_hi + NYH - j) % NYH) * PIECE, PIECE)

    def to_twin(slot, rows):
        return remote(
            panel.at[:, rows, 0:WIDTH], panel.at[:, rows, WIDTH : 2 * WIDTH],
            core_s.at[slot], core_r.at[slot], twin,
        )

    def y_send(j):
        mine = panel.at[:, my_rows, 0:WIDTH]
        return remote(mine, mine, ys_s.at[j], ys_r.at[j], y_peer[j])

    def y_land(j):
        rows = panel.at[:, piece_rows(x, j + 1), 0:WIDTH]
        return remote(rows, rows, ys_s.at[j], ys_r.at[j], y_peer[j])

    def x_send(way, j):
        rows = panel.at[:, piece_rows(x, j), 0:WIDTH]
        return remote(rows, rows, xs_s.at[way, j], xs_r.at[way, j], x_next[way])

    def x_block(way):
        return (x + NX - 1) % NX if way == 0 else (x + 1) % NX

    def x_land(way, j):
        rows = panel.at[:, piece_rows(x_block(way), j), 0:WIDTH]
        return remote(rows, rows, xs_s.at[way, j], xs_r.at[way, j], x_next[way])

    def x_forward(way, j):
        rows = panel.at[way, piece_rows(x_block(way), j), 0:WIDTH]
        return remote(rows, rows, xf_s.at[way, j], xf_r.at[way, j], x_next[way])

    def x_forward_land(way, j):
        rows = panel.at[way, piece_rows((x + 2) % NX, j), 0:WIDTH]
        return remote(rows, rows, xf_s.at[way, j], xf_r.at[way, j], x_next[way])

    for j in range(3):
        y_send(j).start()
    for way in range(2):
        x_send(way, 0).start()
    to_twin(0, my_rows).start()
    w_swap = [
        remote(w_in.at[:, other_cols], wi.at[WIDTH : 2 * WIDTH, :], wx_s.at[0], wx_r.at[0], twin),
        remote(w_out.at[other_cols, :], wo.at[:, WIDTH : 2 * WIDTH], wx_s.at[1], wx_r.at[1], twin),
    ]
    for copy in w_swap:
        copy.start()
    for j in range(3):
        y_land(j).wait_recv()
        for way in range(2):
            x_send(way, j + 1).start()
        to_twin(j + 1, piece_rows(x, j + 1)).start()

    def block_of(k):
        step = jnp.where(k == 2, 3, jnp.where(k == 3, 2, k))
        return (x + step) % NX

    def matmuls(k):
        for j in range(4):
            slot = k * 4 + j
            rows = piece_rows(block_of(k), j)
            landed = panel.at[:, rows, WIDTH : 2 * WIDTH]
            remote(landed, landed, core_s.at[slot], core_r.at[slot], twin).wait_recv()
        rows = at16(block_of(k) * BLOCK, BLOCK)
        part[k, 0] = jnp.dot(panel[0, rows, :], wi[...], preferred_element_type=F32)
        part[k, 1] = nt(panel[1, rows, :], wo[...])

    def rs_copy(way, k, s):
        if s == 0:
            src, dst = rs_out.at[way, k, 0, way], rs_in.at[way, k, 0, way]
        else:
            src, dst = rs_out.at[way, k, s], rs_in.at[way, k, s]
        return remote(src, dst, rs_s.at[way, k, s], rs_r.at[way, k, s], z_next[way])

    def rs_step(k, s):
        for way in range(2):
            target = (z + NZ + (4 - s if way == 0 else s - 4)) % NZ
            rows = at16(target * CHUNK, CHUNK)
            if s > 0:
                rs_copy(way, k, s - 1).wait_recv()
            for array in range(2):
                if s == 0 and array != way:
                    continue
                term = part[k, array, rows, :]
                if s > 1 or (s == 1 and array == way):
                    term = term + rs_in[way, k, s - 1, array].astype(F32)
                rs_out[way, k, s, array] = term.astype(BF16)
            rs_copy(way, k, s).start()

    def y_exchange(k):
        return remote(y_out.at[k], y_in.at[k], ye_s.at[k], ye_r.at[k], partner)

    def rs_end(k):
        rows = at16(z * CHUNK, CHUNK)
        for way in range(2):
            rs_copy(way, k, 3).wait_recv()
        for array in range(2):
            y_out[k, array] = part[k, array, rows, :] + (
                rs_in[0, k, 3, array].astype(F32) + rs_in[1, k, 3, array].astype(F32)
            )
        y_exchange(k).start()

    def ag_copy(way, k, s, origin):
        rows = at16(block_of(k) * BLOCK + origin * CHUNK, CHUNK)
        ref = ah.at[core, way, rows, :] if s == 3 else ah.at[core, :, rows, :]
        return remote(ref, ref, ag_s.at[way, k, s], ag_r.at[way, k, s], z_next[way])

    def ag_origin(way, s):
        return (z + NZ + (-s if way == 0 else s)) % NZ

    def ag_step(k, s):
        for way in range(2):
            if s > 0:
                ag_copy(way, k, s - 1, ag_origin(way, s)).wait_recv()
            ag_copy(way, k, s, ag_origin(way, s)).start()

    def gelu(k):
        y_exchange(k).wait_recv()
        value, grad = activate(y_out[k, 0] + y_in[k, 0], y_out[k, 1] + y_in[k, 1])
        rows = at16(block_of(k) * BLOCK + z * CHUNK, CHUNK)
        ah[core, 0, rows, :] = value
        ah[core, 1, rows, :] = grad
        ag_step(k, 0)

    def half_swap(k, half):
        ref = ah.at[half, :, at16(block_of(k) * BLOCK, BLOCK), :]
        return remote(ref, ref, cf_s.at[k], cf_r.at[k], twin)

    def ag_end(k):
        for way in range(2):
            ag_copy(way, k, 3, ag_origin(way, 4)).wait_recv()
        half_swap(k, core).start()

    x_to = {1: x_next[0], 2: x_next[1], 3: x_far}

    def gx_copy(k):
        return remote(x_out.at[k - 1], x_in.at[k - 1], gx_s.at[k - 1], gx_r.at[k - 1], x_to[k])

    def grad_block(k):
        half_swap(k, other).wait_recv()
        rows = at16(block_of(k) * BLOCK, BLOCK)
        return nt(ah[0, 1, rows, :], w_full[:, 0:HALF]) + nt(
            ah[1, 1, rows, :], w_full[:, HALF:HIDDEN]
        )

    own[2].wait()
    own[3].wait()
    for copy in w_swap:
        copy.wait_recv()
    matmuls(0)
    rs_step(0, 0)
    for j in range(4):
        for way in range(2):
            x_land(way, j).wait_recv()
            x_forward(way, j).start()
            to_twin((1 if way == 1 else 2) * 4 + j, piece_rows(x_block(way), j)).start()
    rs_step(0, 1)
    matmuls(1)
    rs_step(1, 0)
    matmuls(2)
    rs_step(2, 0)
    for j in range(4):
        for way in range(2):
            x_forward_land(way, j).wait_recv()
        to_twin(12 + j, piece_rows((x + 2) % NX, j)).start()
    rs_step(0, 2)
    rs_step(1, 1)
    rs_step(2, 1)
    matmuls(3)
    rs_step(3, 0)
    rs_step(0, 3)
    rs_step(1, 2)
    rs_step(2, 2)
    rs_step(3, 1)
    rs_end(0)
    rs_step(1, 3)
    rs_step(2, 3)
    rs_step(3, 2)
    gelu(0)
    rs_end(1)
    rs_end(2)
    rs_step(3, 3)
    ag_step(0, 1)
    gelu(1)
    gelu(2)
    rs_end(3)
    ag_step(0, 2)
    ag_step(1, 1)
    ag_step(2, 1)
    gelu(3)
    ag_step(1, 2)
    ag_step(2, 2)
    ag_step(3, 1)
    ag_step(1, 3)
    ag_step(2, 3)
    ag_step(3, 2)
    ag_step(0, 3)
    ag_end(1)
    ag_end(2)
    ag_step(3, 3)
    ag_end(0)
    own[4].wait()
    for k in (1, 2):
        x_out[k - 1] = grad_block(k)
        gx_copy(k).start()
    ag_end(3)
    gx[...] = grad_block(0)
    x_out[2] = grad_block(3)
    gx_copy(3).start()

    def gwo_part(half):
        rows = pl.ds(half * HALF, HALF)
        gwo_stage[rows, :] = tn(ah[half, 0], panel[1, :, 0:WIDTH]).astype(BF16)
        copy = pltpu.make_async_copy(
            gwo_stage.at[rows, :], grad_w_out.at[rows, :], local_sem.at[5 + half]
        )
        copy.start()
        return copy

    def gwi_part(half):
        cols = pl.ds(half * HALF, HALF)
        gwi_stage[:, cols] = tn(panel[0, :, 0:WIDTH], ah[half, 1]).astype(BF16)
        copy = pltpu.make_async_copy(
            gwi_stage.at[:, cols], grad_w_in.at[:, cols], local_sem.at[7 + half]
        )
        copy.start()
        return copy

    written = [gwo_part(0), gwo_part(1)]
    for k in (1, 2, 3):
        gx_copy(k).wait_recv()
        gx[...] += x_in[k - 1]

    def gy_copy(j):
        return remote(gy_out.at[j], gy_in.at[j], gy_s.at[j], gy_r.at[j], y_peer[j])

    for j in range(3):
        gy_out[j] = gx[at16(((y_hi + j + 1) % NYH) * PIECE, PIECE), :]
        gy_copy(j).start()
    written += [gwi_part(0), gwi_part(1)]
    total = gx[at16(y_hi * PIECE, PIECE), :]
    for j in range(3):
        gy_copy(j).wait_recv()
        total = total + gy_in[j]
    gi_stage[...] = total.astype(BF16)
    last = pltpu.make_async_copy(gi_stage, grad_inputs, local_sem.at[9])
    last.start()

    for j in range(3):
        y_send(j).wait_send()
        gy_copy(j).wait_send()
    for way in range(2):
        for j in range(4):
            x_send(way, j).wait_send()
            x_forward(way, j).wait_send()
    for k in range(4):
        for j in range(4):
            to_twin(k * 4 + j, piece_rows(block_of(k), j)).wait_send()
        for s in range(4):
            for way in range(2):
                rs_copy(way, k, s).wait_send()
                ag_copy(way, k, s, ag_origin(way, s)).wait_send()
        y_exchange(k).wait_send()
        half_swap(k, core).wait_send()
    for k in (1, 2, 3):
        gx_copy(k).wait_send()
    for copy in w_swap:
        copy.wait_send()
    for copy in written:
        copy.wait()
    last.wait()


def body(inputs, out_grad, w_in, w_out):
    any_space = pl.BlockSpec(memory_space=pl.ANY)
    dma = pltpu.SemaphoreType.DMA
    return pl.pallas_call(
        kernel,
        out_shape=(
            jax.ShapeDtypeStruct((PIECE, WIDTH), BF16),
            jax.ShapeDtypeStruct((WIDTH, HIDDEN), BF16),
            jax.ShapeDtypeStruct((HIDDEN, WIDTH), BF16),
        ),
        in_specs=[any_space] * 4,
        out_specs=(any_space,) * 3,
        scratch_shapes=[
            pltpu.VMEM((2, TOKENS, 2 * WIDTH), BF16),
            pltpu.VMEM((2 * WIDTH, HALF), BF16),
            pltpu.VMEM((HALF, 2 * WIDTH), BF16),
            pltpu.VMEM((WIDTH, HIDDEN), BF16),
            pltpu.VMEM((4, 2, BLOCK, HALF), F32),
            pltpu.VMEM((2, 4, 4, 2, CHUNK, HALF), BF16),
            pltpu.VMEM((2, 4, 4, 2, CHUNK, HALF), BF16),
            pltpu.VMEM((4, 2, CHUNK, HALF), F32),
            pltpu.VMEM((4, 2, CHUNK, HALF), F32),
            pltpu.VMEM((2, 2, TOKENS, HALF), BF16),
            pltpu.VMEM((3, BLOCK, WIDTH), F32),
            pltpu.VMEM((3, BLOCK, WIDTH), F32),
            pltpu.VMEM((BLOCK, WIDTH), F32),
            pltpu.VMEM((3, PIECE, WIDTH), F32),
            pltpu.VMEM((3, PIECE, WIDTH), F32),
            pltpu.VMEM((PIECE, WIDTH), BF16),
            pltpu.VMEM((WIDTH, HIDDEN), BF16),
            pltpu.VMEM((HIDDEN, WIDTH), BF16),
            dma((10,)),
            dma((16,)), dma((16,)),
            dma((2,)), dma((2,)),
            dma((3,)), dma((3,)),
            dma((2, 4)), dma((2, 4)),
            dma((2, 4)), dma((2, 4)),
            dma((2, 4, 4)), dma((2, 4, 4)),
            dma((4,)), dma((4,)),
            dma((2, 4, 4)), dma((2, 4, 4)),
            dma((4,)), dma((4,)),
            dma((3,)), dma((3,)),
            dma((3,)), dma((3,)),
        ],
        compiler_params=pltpu.CompilerParams(
            collective_id=0, has_side_effects=True, vmem_limit_bytes=40 << 20
        ),
        cost_estimate=pl.CostEstimate(
            flops=6 * 10**9, bytes_accessed=5 * 10**6, transcendentals=10**6
        ),
        name="ffn_backward",
    )(inputs, out_grad, w_in, w_out)


def solution(mesh):
    return jax.shard_map(
        body,
        mesh=mesh,
        in_specs=(P("col", "row"), P("col", "row"), P("row", "col"), P("col", "row")),
        out_specs=(P("col", "row"), P("row", "col"), P("col", "row")),
        check_vma=False,
    )
```

time: 453 us -> 92 us (0.20)
  waiting for transfers between devices: 340 us -> 0 us
  Pallas kernels: 0 us -> 84.4 us
  blocking collectives: 75.4 us -> 0 us
  matrix products: 14.8 us -> 0 us
  between operations: 14.1 us -> 0.65 us
  other arithmetic: 5.31 us -> 0 us
    psum x1 -> x0, waiting for transfers between devices: 261 us -> none  [body(): preact, upstream = lax.psum((preact_part, upstream_part), 'row')]
    pallas_call x0 -> x1, Pallas kernels: none -> 84.4 us  [body(): pl.pallas_call(kernel, out_shape=(jax.ShapeDtypeStruct((PIECE, WIDTH), BF...]
    reduce_scatter x1 -> x0, waiting for transfers between devices: 79.4 us -> none  [body(): lax.psum_scatter(right_trans(hidden_grad, w_in), 'col', scatter_dimension...]
    all_gather x2 -> x0, blocking collectives: 75.4 us -> none  [the longest x1 41 us: body(): lax.all_gather(inputs, 'col', axis=0, tiled=True)]
    dot_general x5 -> x0, matrix products: 14.8 us -> none  [the longest x2 6.31 us: left_trans(): lax.dot_general(left, right, (((0,), (0,)), ((), ())), preferred_element_...]
    convert_element_type x2 -> x0, other arithmetic: 5.31 us -> none  [the longest x1 3.9 us: activate(): hidden_grad = (upstream * gelu_slope(preact)).astype(jnp.bfloat16)]
  transfers between devices with their start and end apart: 2 -> 0, of which waited for: 2 -> 0; matrix products, arithmetic and copies ran while one was open for 2% -> 0% of each run, Pallas kernels for 0% -> 0%
where the time goes in v1:
time: 92 us; the launch traced here: 91.7 us
  Pallas kernels  84.4 us (92%)
  local copies, waits for them, and re-layouts  6.64 us (7%)
    pallas_call x1, Pallas kernels, body(): pl.pallas_call(kernel, out_shape=(jax.ShapeDtypeStruct((PIECE, WIDTH), BF...  84.4 us
    unnamed x11, local copies, waits for them, and re-layouts  6.64 us

profile of v1, /device:TPU:1, one launch (start us, length us, event | category | flops | bytes accessed | tf_op | source)
XLA Modules:
  0.0 91.7 jit_solution(2327362734075335724)
XLA Ops:
  0.6 0.0 copy-start
  0.6 1.3 %copy-done = bf16[384,1536]{1,0:T(8,128)(2,1)S(1)} copy-done((bf16[384,1536]{1,0:T(8,128)(2,1)S(1)}, bf16[384,1536]{1,0:T(8,128)(2,1)}, u32[]{:S(2)}) %copy-start) | copy-done | bytes 1179672
  1.9 0.0 copy-start.1
  1.9 1.3 %copy-done.1 = bf16[1536,384]{1,0:T(8,128)(2,1)S(1)} copy-done((bf16[1536,384]{1,0:T(8,128)(2,1)S(1)}, bf16[1536,384]{1,0:T(8,128)(2,1)}, u32[]{:S(2)}) %copy-start.1) | copy-done | bytes 1179672
  3.2 0.0 copy-start.2
  3.2 0.7 copy-done.2
  3.9 0.0 copy-start.3
  3.9 0.7 copy-done.3
  4.6 84.4 %ffn_backward.1 = (bf16[32,384]{1,0:T(8,128)(2,1)S(1)}, bf16[384,1536]{1,0:T(8,128)(2,1)S(1)}, bf16[1536,384]{1,0:T(8,128)(2,1)S(1)}) custom-call(bf16[32,384]{1,0:T(8,128)(2,1)S(1)} %copy-done.2, bf16[32,384]{1,0:T(8,128)(2,1)S(1)} %copy-done.3, bf16[384,1536]{1,0:T(8,128)(2,1)S(1)} %copy-done, bf16[1536,384]{1,0:T(8,128)(2,1)S(1)} %copy-done.1), custom_call_target="tpu_custom_call" | custom-call | flops 6000000000 | bytes 5000000 | tf_op jit(solution)/shard_map/ffn_backward/pallas_call | solution.py:379
  89.1 0.6 copy.10
  89.7 1.0 %copy.11 = bf16[384,1536]{1,0:T(8,128)(2,1)} copy(bf16[384,1536]{1,0:T(8,128)(2,1)S(1)} %get-tuple-element.7) | data formatting | bytes 2359296
  90.7 1.0 %copy.12 = bf16[1536,384]{1,0:T(8,128)(2,1)} copy(bf16[1536,384]{1,0:T(8,128)(2,1)S(1)} %get-tuple-element.8) | data formatting | bytes 2359296
Async XLA Ops:
  0.6 1.3 %copy-start = (bf16[384,1536]{1,0:T(8,128)(2,1)S(1)}, bf16[384,1536]{1,0:T(8,128)(2,1)}, u32[]{:S(2)}) copy-start(bf16[384,1536]{1,0:T(8,128)(2,1)} %w_in.1) | copy-start | bytes 3538948
  1.9 1.3 %copy-start.1 = (bf16[1536,384]{1,0:T(8,128)(2,1)S(1)}, bf16[1536,384]{1,0:T(8,128)(2,1)}, u32[]{:S(2)}) copy-start(bf16[1536,384]{1,0:T(8,128)(2,1)} %w_out.1) | copy-start | bytes 3538948
  3.2 0.7 copy-start.2
  3.9 0.7 copy-start.3

commit v2 on v0

v2 whole, which is shorter than its diff:
```python
import functools

import jax
import jax.numpy as jnp
from jax import lax
from jax.experimental import pallas as pl
from jax.experimental.pallas import tpu as pltpu
from jax.sharding import PartitionSpec as P

MESH = pl.DeviceIdType.MESH
BF16 = jnp.bfloat16
F32 = jnp.float32

slope_const = 0.7978845608028654
cubic_coef = 0.044715

NX, NYH, NYL, NZ = 4, 4, 2, 8
TOKENS = 512
BLOCK = TOKENS // 4
PIECE = TOKENS // (NX * NYH)
CHUNK = BLOCK // NZ
WIDTH = 384
HIDDEN = 1536
HALF = HIDDEN // 2

DY = (0, 1, 3, 2)

SEMAPHORES = {
    "core": (4, 4),
    "wx": (2,),
    "ys": (3,),
    "xs": (3, 4),
    "rs": (2, 4, 4),
    "ye": (4,),
    "ag": (2, 4, 4),
    "cf": (4,),
    "gx": (3, 4),
    "gy": (3,),
}


def nt(left, right):
    return lax.dot_general(
        left, right, (((1,), (1,)), ((), ())), preferred_element_type=F32
    )


def tn(left, right):
    return lax.dot_general(
        left, right, (((0,), (0,)), ((), ())), preferred_element_type=F32
    )


def activate(preact, upstream):
    square = preact * preact
    inner = slope_const * (preact + cubic_coef * square * preact)
    tanh_val = jnp.tanh(inner)
    deriv = slope_const * (1.0 + 3.0 * cubic_coef * square)
    value = 0.5 * preact * (1.0 + tanh_val)
    slope = 0.5 * (1.0 + tanh_val) + 0.5 * preact * (1.0 - tanh_val * tanh_val) * deriv
    return value.astype(BF16), (upstream * slope).astype(BF16)


def kernel(
    inputs, out_grad, w_in, w_out,
    grad_inputs, grad_w_in, grad_w_out,
    panel, wi, wo, w_full, wo_other, part, rs_out, rs_in, y_out, y_in, ah,
    g, gx_in, gy_out, gy_in, local_sem, *pairs,
):
    row, col = lax.axis_index("row"), lax.axis_index("col")
    y_lo, z, core = row // 16, (row // 2) % 8, row % 2
    x, y_hi = col // 4, col % 4
    other = 1 - core

    def device(y_lo=y_lo, z=z, core=core, x=x, y_hi=y_hi):
        return ((y_lo * NZ + z) * 2 + core, x * NYH + y_hi)

    twin = device(core=other)
    partner = device(y_lo=1 - y_lo)
    z_next = (device(z=(z + 1) % NZ), device(z=(z + NZ - 1) % NZ))
    x_peer = [None, *(device(x=(x + d) % NX) for d in range(1, NX))]
    y_peer = [None, *(device(y_hi=(y_hi + d) % NYH) for d in range(1, NYH))]

    sems = {kind: pairs[2 * i : 2 * i + 2] for i, kind in enumerate(SEMAPHORES)}
    sent = []

    def remote(src, dst, kind, index, to):
        send, recv = sems[kind]
        return pltpu.make_async_remote_copy(
            src_ref=src, dst_ref=dst, send_sem=send.at[index], recv_sem=recv.at[index],
            device_id=to, device_id_type=MESH,
        )

    def start(copy):
        copy.start()
        sent.append(copy)

    half_cols = pl.ds(pl.multiple_of(core * HALF, 128), HALF)
    other_cols = pl.ds(pl.multiple_of(other * HALF, 128), HALF)
    own = [
        pltpu.make_async_copy(inputs, panel.at[0, 0:PIECE, 0:WIDTH], local_sem.at[0]),
        pltpu.make_async_copy(out_grad, panel.at[1, 0:PIECE, 0:WIDTH], local_sem.at[1]),
        pltpu.make_async_copy(w_in.at[:, half_cols], wi.at[0:WIDTH, :], local_sem.at[2]),
        pltpu.make_async_copy(w_out.at[half_cols, :], wo.at[:, 0:WIDTH], local_sem.at[3]),
        pltpu.make_async_copy(w_in, w_full, local_sem.at[4]),
        pltpu.make_async_copy(w_out.at[other_cols, :], wo_other, local_sem.at[5]),
    ]
    for copy in own:
        copy.start()

    barrier = pltpu.get_barrier_semaphore()
    greeted = [twin, partner, *z_next, *x_peer[1:], *y_peer[1:]]
    for peer in greeted:
        pl.semaphore_signal(barrier, inc=1, device_id=peer, device_id_type=MESH)
    pl.semaphore_wait(barrier, len(greeted))

    def piece_rows(dx, dy):
        slot = 4 * DY.index(dy) + dx
        return slice(slot * PIECE, (slot + 1) * PIECE)

    def piece(dx, dy):
        return panel.at[:, piece_rows(dx, dy), 0:WIDTH]

    def to_twin(dx, dy):
        there = panel.at[:, piece_rows(dx, dy), WIDTH : 2 * WIDTH]
        return remote(piece(dx, dy), there, "core", (dx, dy), twin)

    def y_copy(d):
        return remote(piece(0, 0), piece(0, NYH - d), "ys", (d - 1,), y_peer[d])

    def x_copy(d, dy):
        return remote(piece(0, dy), piece(NX - d, dy), "xs", (d - 1, dy), x_peer[d])

    def own_ready(dy):
        for d in (1, 3, 2):
            start(x_copy(d, dy))
        start(to_twin(0, dy))

    def y_arrive(d):
        y_copy(d).wait_recv()
        own_ready(NYH - d)

    def x_arrive(dy):
        for d in (1, 3, 2):
            x_copy(d, dy).wait_recv()
            start(to_twin(NX - d, dy))

    def matmuls(k):
        for dx in range(NX):
            to_twin(dx, DY[k]).wait_recv()
        rows = slice(k * BLOCK, (k + 1) * BLOCK)
        part[k, 0] = jnp.dot(panel[0, rows, :], wi[...], preferred_element_type=F32)
        part[k, 1] = nt(panel[1, rows, :], wo[...])

    def chunk(start):
        return pl.ds(pl.multiple_of(start, 16), CHUNK)

    def rs_copy(way, k, s):
        if s == 0:
            src, dst = rs_out.at[way, k, 0, way], rs_in.at[way, k, 0, way]
        else:
            src, dst = rs_out.at[way, k, s], rs_in.at[way, k, s]
        return remote(src, dst, "rs", (way, k, s), z_next[way])

    def rs_step(k, s):
        for way in range(2):
            target = (z + NZ + (4 - s if way == 0 else s - 4)) % NZ
            rows = chunk(target * CHUNK)
            if s > 0:
                rs_copy(way, k, s - 1).wait_recv()
            for array in range(2):
                if s == 0 and array != way:
                    continue
                term = part[k, array, rows, :]
                if s > 1 or (s == 1 and array == way):
                    term = term + rs_in[way, k, s - 1, array].astype(F32)
                rs_out[way, k, s, array] = term.astype(BF16)
            start(rs_copy(way, k, s))

    def y_exchange(k):
        return remote(y_out.at[k], y_in.at[k], "ye", (k,), partner)

    def rs_end(k):
        rows = chunk(z * CHUNK)
        for way in range(2):
            rs_copy(way, k, 3).wait_recv()
        for array in range(2):
            y_out[k, array] = part[k, array, rows, :] + (
                rs_in[0, k, 3, array].astype(F32) + rs_in[1, k, 3, array].astype(F32)
            )
        start(y_exchange(k))

    def ag_copy(way, k, s, origin):
        rows = chunk(k * BLOCK + origin * CHUNK)
        ref = ah.at[core, way, rows, :] if s == 3 else ah.at[core, :, rows, :]
        return remote(ref, ref, "ag", (way, k, s), z_next[way])

    def ag_origin(way, s):
        return (z + NZ + (-s if way == 0 else s)) % NZ

    def ag_step(k, s):
        for way in range(2):
            if s > 0:
                ag_copy(way, k, s - 1, ag_origin(way, s)).wait_recv()
            start(ag_copy(way, k, s, ag_origin(way, s)))

    def gelu(k):
        y_exchange(k).wait_recv()
        value, grad = activate(y_out[k, 0] + y_in[k, 0], y_out[k, 1] + y_in[k, 1])
        rows = chunk(k * BLOCK + z * CHUNK)
        ah[core, 0, rows, :] = value
        ah[core, 1, rows, :] = grad
        ag_step(k, 0)

    def half_swap(k, half):
        ref = ah.at[half, :, k * BLOCK : (k + 1) * BLOCK, :]
        return remote(ref, ref, "cf", (k,), twin)

    def ag_end(k):
        for way in range(2):
            ag_copy(way, k, 3, ag_origin(way, 4)).wait_recv()
        start(half_swap(k, core))

    def g_piece(dx, dy):
        return g.at[DY.index(dy), dx * PIECE : (dx + 1) * PIECE]

    def gx_copy(dx, dy):
        return remote(g_piece(dx, dy), gx_in.at[dx - 1, dy], "gx", (dx - 1, dy), x_peer[dx])

    def grad_block(k):
        half_swap(k, other).wait_recv()
        rows = slice(k * BLOCK, (k + 1) * BLOCK)
        g[k] = nt(ah[0, 1, rows, :], w_full[:, 0:HALF]) + nt(
            ah[1, 1, rows, :], w_full[:, HALF:HIDDEN]
        )
        for dx in (2, 1, 3):
            start(gx_copy(dx, DY[k]))

    def x_sum(dy):
        total = g_piece(0, dy)[...]
        for dx in range(1, NX):
            gx_copy(dx, dy).wait_recv()
            total = total + gx_in[dx - 1, dy]
        return total

    def gy_copy(dy):
        return remote(gy_out.at[dy - 1], gy_in.at[dy - 1], "gy", (dy - 1,), y_peer[dy])

    def y_part(dy):
        gy_out[dy - 1] = x_sum(dy)
        start(gy_copy(dy))

    def weight_grads(half):
        cols = slice(half * HALF, (half + 1) * HALF)
        grad_w_out[cols, :] = tn(ah[half, 0], panel[1, :, 0:WIDTH]).astype(BF16)
        grad_w_in[:, cols] = tn(panel[0, :, 0:WIDTH], ah[half, 1]).astype(BF16)

    own[0].wait()
    own[1].wait()
    for d in (1, 3, 2):
        start(y_copy(d))
    own_ready(0)
    own[4].wait()
    own[5].wait()
    w_swap = [
        remote(w_full.at[:, other_cols], wi.at[WIDTH : 2 * WIDTH, :], "wx", (0,), twin),
        remote(wo_other, wo.at[:, WIDTH : 2 * WIDTH], "wx", (1,), twin),
    ]
    for copy in w_swap:
        start(copy)
    own[2].wait()
    own[3].wait()
    x_arrive(0)
    y_arrive(1)
    y_arrive(3)
    for copy in w_swap:
        copy.wait_recv()
    matmuls(0)
    rs_step(0, 0)
    y_arrive(2)
    rs_step(0, 1)
    x_arrive(3)
    matmuls(2)
    x_arrive(1)
    rs_step(2, 0)
    matmuls(1)
    x_arrive(2)
    rs_step(1, 0)
    rs_step(0, 2)
    rs_step(2, 1)
    matmuls(3)
    rs_step(3, 0)
    rs_step(1, 1)
    rs_step(0, 3)
    rs_step(2, 2)
    rs_step(3, 1)
    rs_step(1, 2)
    rs_end(0)
    rs_step(2, 3)
    rs_step(3, 2)
    rs_step(1, 3)
    rs_end(2)
    gelu(0)
    rs_step(3, 3)
    rs_end(1)
    ag_step(0, 1)
    gelu(2)
    rs_end(3)
    gelu(1)
    ag_step(0, 2)
    ag_step(2, 1)
    gelu(3)
    ag_step(1, 1)
    ag_step(0, 3)
    ag_step(2, 2)
    ag_step(3, 1)
    ag_step(1, 2)
    ag_end(0)
    ag_step(2, 3)
    grad_block(0)
    ag_step(3, 2)
    ag_step(1, 3)
    ag_end(2)
    ag_step(3, 3)
    grad_block(2)
    ag_end(1)
    grad_block(1)
    ag_end(3)
    grad_block(3)
    y_part(3)
    weight_grads(0)
    weight_grads(1)
    y_part(1)
    y_part(2)
    total = x_sum(0)
    for dy in range(1, NYH):
        gy_copy(dy).wait_recv()
        total = total + gy_in[dy - 1]
    grad_inputs[...] = total.astype(BF16)

    for copy in sent:
        copy.wait_send()


def store(*refs):
    half = len(refs) // 2
    sems = refs[-1]
    copies = [
        pltpu.make_async_copy(refs[i], refs[half + i], sems.at[i]) for i in range(half)
    ]
    for copy in copies:
        copy.start()
    for copy in copies:
        copy.wait()


def body(inputs, out_grad, w_in, w_out):
    hbm = pl.BlockSpec(memory_space=pltpu.HBM)
    vmem = pl.BlockSpec(memory_space=pltpu.VMEM)
    dma = pltpu.SemaphoreType.DMA
    shapes = ((PIECE, WIDTH), (WIDTH, HIDDEN), (HIDDEN, WIDTH))
    results = pl.pallas_call(
        kernel,
        out_shape=tuple(pltpu.VMEM(shape, BF16) for shape in shapes),
        in_specs=[hbm] * 4,
        out_specs=(vmem,) * 3,
        scratch_shapes=[
            pltpu.VMEM((2, TOKENS, 2 * WIDTH), BF16),
            pltpu.VMEM((2 * WIDTH, HALF), BF16),
            pltpu.VMEM((HALF, 2 * WIDTH), BF16),
            pltpu.VMEM((WIDTH, HIDDEN), BF16),
            pltpu.VMEM((HALF, WIDTH), BF16),
            pltpu.VMEM((4, 2, BLOCK, HALF), F32),
            pltpu.VMEM((2, 4, 4, 2, CHUNK, HALF), BF16),
            pltpu.VMEM((2, 4, 4, 2, CHUNK, HALF), BF16),
            pltpu.VMEM((4, 2, CHUNK, HALF), F32),
            pltpu.VMEM((4, 2, CHUNK, HALF), F32),
            pltpu.VMEM((2, 2, TOKENS, HALF), BF16),
            pltpu.VMEM((4, BLOCK, WIDTH), F32),
            pltpu.VMEM((3, 4, PIECE, WIDTH), F32),
            pltpu.VMEM((3, PIECE, WIDTH), F32),
            pltpu.VMEM((3, PIECE, WIDTH), F32),
            dma((6,)),
            *(dma(shape) for shape in SEMAPHORES.values() for _ in range(2)),
        ],
        compiler_params=pltpu.CompilerParams(
            collective_id=0, has_side_effects=True, vmem_limit_bytes=60 << 20
        ),
        cost_estimate=pl.CostEstimate(
            flops=6 * 10**9, bytes_accessed=5 * 10**6, transcendentals=10**6
        ),
        name="ffn_backward",
    )(inputs, out_grad, w_in, w_out)
    return pl.pallas_call(
        store,
        out_shape=tuple(jax.ShapeDtypeStruct(shape, BF16) for shape in shapes),
        in_specs=[pl.BlockSpec(memory_space=pl.ANY)] * 3,
        out_specs=(pl.BlockSpec(memory_space=pl.ANY),) * 3,
        scratch_shapes=[dma((3,))],
        compiler_params=pltpu.CompilerParams(vmem_limit_bytes=1 << 20),
        name="store_results",
    )(*results)


def solution(mesh):
    return jax.shard_map(
        body,
        mesh=mesh,
        in_specs=(P("col", "row"), P("col", "row"), P("row", "col"), P("col", "row")),
        out_specs=(P("col", "row"), P("row", "col"), P("col", "row")),
        check_vma=False,
    )
```

time: 453 us -> 82 us (0.18)
  the two profiles are of different devices: /device:TPU:1 before, /device:TPU:9 now
where the time goes in v2:
time: 82 us; the launch traced here: 81.9 us
  Pallas kernels  81.3 us (99%)
    pallas_call x1, Pallas kernels, body(): pl.pallas_call(kernel, out_shape=tuple((pltpu.VMEM(shape, BF16) for shape...  79.8 us

profile of v2, /device:TPU:9, one launch (start us, length us, event | category | flops | bytes accessed | tf_op | source)
XLA Modules:
  0.0 81.9 jit_solution(2193815178629608886)
XLA Ops:
  0.6 79.8 %ffn_backward.1 = (bf16[32,384]{1,0:T(8,128)(2,1)S(1)}, bf16[384,1536]{1,0:T(8,128)(2,1)S(1)}, bf16[1536,384]{1,0:T(8,128)(2,1)S(1)}) custom-call(bf16[32,384]{1,0:T(8,128)(2,1)} %inputs.1, bf16[32,384]{1,0:T(8,128)(2,1)} %out_grad.1, bf16[384,1536]{1,0:T(8,128)(2,1)} %w_in.1, bf16[1536,384]{1,0:T(8,128)(2,1)} %w_out.1), custom_call_target="tpu_custom_call" | custom-call | flops 6000000000 | bytes 5000000 | tf_op jit(solution)/shard_map/ffn_backward/pallas_call | solution.py:362
  80.5 1.4 %store_results.1 = (bf16[32,384]{1,0:T(8,128)(2,1)}, bf16[384,1536]{1,0:T(8,128)(2,1)}, bf16[1536,384]{1,0:T(8,128)(2,1)}) custom-call(bf16[32,384]{1,0:T(8,128)(2,1)S(1)} %get-tuple-element.6.refs_0_, bf16[384,1536]{1,0:T(8,128)(2,1)S(1)} %get-tuple-element.7.refs_1_, bf16[1536,384]{1,0:T(8,128)(2,1)S(1)} %get-tuple-element.8.refs_2_), custom_call_target="tpu_custom_call" | custom-call | tf_op jit(solution)/shard_map/store_results/pallas_call | solution.py:394

commit v3 on v2

v3 whole, which is shorter than its diff:
```python
import functools

import jax
import jax.numpy as jnp
from jax import lax
from jax.experimental import pallas as pl
from jax.experimental.pallas import tpu as pltpu
from jax.sharding import PartitionSpec as P

MESH = pl.DeviceIdType.MESH
BF16 = jnp.bfloat16
F32 = jnp.float32

slope_const = 0.7978845608028654
cubic_coef = 0.044715

NX, NYH, NYL, NZ = 4, 4, 2, 8
TOKENS = 512
BLOCK = TOKENS // 4
PIECE = TOKENS // (NX * NYH)
CHUNK = BLOCK // NZ
WIDTH = 384
HIDDEN = 1536
HALF = HIDDEN // 2

DY = (0, 1, 3, 2)

SEMAPHORES = {
    "core": (2, 4, 4),
    "wx": (2,),
    "ys": (2, 2),
    "yf": (2,),
    "xs": (2, 3, 4),
    "rs": (2, 4, 4, 2),
    "ye": (4, 2),
    "ag": (2, 4, 4, 2),
    "cf": (4, 2),
    "gx": (3, 4),
    "gy": (3,),
}


def nt(left, right):
    return lax.dot_general(
        left, right, (((1,), (1,)), ((), ())), preferred_element_type=F32
    )


def tn(left, right):
    return lax.dot_general(
        left, right, (((0,), (0,)), ((), ())), preferred_element_type=F32
    )


def activate(preact, upstream):
    square = preact * preact
    inner = slope_const * (preact + cubic_coef * square * preact)
    tanh_val = jnp.tanh(inner)
    deriv = slope_const * (1.0 + 3.0 * cubic_coef * square)
    value = 0.5 * preact * (1.0 + tanh_val)
    slope = 0.5 * (1.0 + tanh_val) + 0.5 * preact * (1.0 - tanh_val * tanh_val) * deriv
    return value.astype(BF16), (upstream * slope).astype(BF16)


def kernel(
    inputs, out_grad, w_in, w_out,
    grad_inputs, grad_w_in, grad_w_out,
    panel, wi, wo, w_full, wo_other, part, rs_out, rs_in, y_out, y_in, ah,
    g, gx_in, gy_out, gy_in, g_sent, gy_far, local_sem, *pairs,
):
    row, col = lax.axis_index("row"), lax.axis_index("col")
    y_lo, z, core = row // 16, (row // 2) % 8, row % 2
    x, y_hi = col // 4, col % 4
    other = 1 - core

    def device(y_lo=y_lo, z=z, core=core, x=x, y_hi=y_hi):
        return ((y_lo * NZ + z) * 2 + core, x * NYH + y_hi)

    twin = device(core=other)
    partner = device(y_lo=1 - y_lo)
    z_next = (device(z=(z + 1) % NZ), device(z=(z + NZ - 1) % NZ))
    z_over = (device(z=(z + 2) % NZ), device(z=(z + NZ - 2) % NZ))
    x_peer = [None, *(device(x=(x + d) % NX) for d in range(1, NX))]
    y_peer = [None, *(device(y_hi=(y_hi + d) % NYH) for d in range(1, NYH))]

    sems = {kind: pairs[2 * i : 2 * i + 2] for i, kind in enumerate(SEMAPHORES)}
    sent = []

    def remote(src, dst, kind, index, to):
        send, recv = sems[kind]
        return pltpu.make_async_remote_copy(
            src_ref=src, dst_ref=dst, send_sem=send.at[index], recv_sem=recv.at[index],
            device_id=to, device_id_type=MESH,
        )

    def start(copy):
        copy.start()
        sent.append(copy)

    half_cols = pl.ds(pl.multiple_of(core * HALF, 128), HALF)
    other_cols = pl.ds(pl.multiple_of(other * HALF, 128), HALF)
    own = [
        pltpu.make_async_copy(inputs, panel.at[0, 0:PIECE, 0:WIDTH], local_sem.at[0]),
        pltpu.make_async_copy(out_grad, panel.at[1, 0:PIECE, 0:WIDTH], local_sem.at[1]),
        pltpu.make_async_copy(w_in.at[:, half_cols], wi.at[0:WIDTH, :], local_sem.at[2]),
        pltpu.make_async_copy(w_out.at[half_cols, :], wo.at[:, 0:WIDTH], local_sem.at[3]),
        pltpu.make_async_copy(w_in, w_full, local_sem.at[4]),
        pltpu.make_async_copy(w_out.at[other_cols, :], wo_other, local_sem.at[5]),
    ]
    for copy in own:
        copy.start()

    barrier = pltpu.get_barrier_semaphore()
    greeted = [twin, partner, *z_next, *z_over, *x_peer[1:], *y_peer[1:]]
    for peer in greeted:
        pl.semaphore_signal(barrier, inc=1, device_id=peer, device_id_type=MESH)
    pl.semaphore_wait(barrier, len(greeted))

    def piece_rows(dx, dy):
        slot = 4 * DY.index(dy) + dx
        return slice(slot * PIECE, (slot + 1) * PIECE)

    def piece(dx, dy, a):
        return panel.at[a, piece_rows(dx, dy), 0:WIDTH]

    def to_twin(dx, dy, a):
        there = panel.at[a, piece_rows(dx, dy), WIDTH : 2 * WIDTH]
        return remote(piece(dx, dy, a), there, "core", (a, dx, dy), twin)

    def y_copy(d, a):
        return remote(piece(0, 0, a), piece(0, NYH - d, a), "ys", (a, d // 2), y_peer[d])

    def y_forward(a):
        d = 1 if a == 0 else 3
        return remote(piece(0, NYH - d, a), piece(0, 2, a), "yf", (a,), y_peer[d])

    def x_copy(d, dy, a):
        return remote(piece(0, dy, a), piece(NX - d, dy, a), "xs", (a, d - 1, dy), x_peer[d])

    def own_ready(dy, a):
        for d in (1, 3, 2):
            start(x_copy(d, dy, a))
        start(to_twin(0, dy, a))

    def y_arrive(d, a):
        if d == 2:
            y_forward(a).wait_recv()
        else:
            y_copy(d, a).wait_recv()
            if d == (1 if a == 0 else 3):
                start(y_forward(a))
        own_ready(NYH - d, a)

    def x_arrive(dy, a):
        for d in (1, 3, 2):
            x_copy(d, dy, a).wait_recv()
            start(to_twin(NX - d, dy, a))

    def matmuls(k, a):
        for dx in range(NX):
            to_twin(dx, DY[k], a).wait_recv()
        rows = slice(k * BLOCK, (k + 1) * BLOCK)
        if a == 0:
            part[k, 0] = jnp.dot(panel[0, rows, :], wi[...], preferred_element_type=F32)
        else:
            part[k, 1] = nt(panel[1, rows, :], wo[...])

    def chunk(start):
        return pl.ds(pl.multiple_of(start, 16), CHUNK)

    def rs_copy(way, k, s, a):
        to = z_over[way] if s == 0 else z_next[way]
        return remote(
            rs_out.at[way, k, s, a], rs_in.at[way, k, s, a], "rs", (way, k, s, a), to
        )

    def rs_step(k, s, a):
        for way in range(2):
            if s == 0 and way != a:
                continue
            target = (z + NZ + (4 - s if way == 0 else s - 4)) % NZ
            term = part[k, a, chunk(target * CHUNK), :]
            for earlier in {2: (1, 0) if way == a else (1,), 3: (2,)}.get(s, ()):
                rs_copy(way, k, earlier, a).wait_recv()
                term = term + rs_in[way, k, earlier, a].astype(F32)
            rs_out[way, k, s, a] = term.astype(BF16)
            start(rs_copy(way, k, s, a))

    def y_exchange(k, a):
        return remote(y_out.at[k, a], y_in.at[k, a], "ye", (k, a), partner)

    def rs_end(k, a):
        for way in range(2):
            rs_copy(way, k, 3, a).wait_recv()
        y_out[k, a] = part[k, a, chunk(z * CHUNK), :] + (
            rs_in[0, k, 3, a].astype(F32) + rs_in[1, k, 3, a].astype(F32)
        )
        start(y_exchange(k, a))

    def ag_copy(way, k, s, a, origin):
        ref = ah.at[core, a, chunk(k * BLOCK + origin * CHUNK), :]
        to = z_over[way] if s == 3 else z_next[way]
        return remote(ref, ref, "ag", (way, k, s, a), to)

    def ag_origin(way, s):
        return (z + NZ + (-s if way == 0 else s)) % NZ

    def ag_step(k, s, a):
        for way in range(2):
            if s > 0:
                ag_copy(way, k, s - 1, a, ag_origin(way, s)).wait_recv()
            start(ag_copy(way, k, s, a, ag_origin(way, s)))
            if s == 2 and way == a:
                start(ag_copy(way, k, 3, a, ag_origin(way, 2)))

    def gelu(k):
        for a in range(2):
            y_exchange(k, a).wait_recv()
        value, grad = activate(y_out[k, 0] + y_in[k, 0], y_out[k, 1] + y_in[k, 1])
        rows = chunk(k * BLOCK + z * CHUNK)
        ah[core, 1, rows, :] = grad
        ag_step(k, 0, 1)
        ah[core, 0, rows, :] = value
        ag_step(k, 0, 0)

    def half_swap(k, a, half):
        ref = ah.at[half, a, k * BLOCK : (k + 1) * BLOCK, :]
        return remote(ref, ref, "cf", (k, a), twin)

    def ag_end(k, a):
        for way in range(2):
            ag_copy(way, k, 2, a, ag_origin(way, 3)).wait_recv()
        ag_copy(a, k, 3, a, ag_origin(a, 4)).wait_recv()
        start(half_swap(k, a, core))

    def g_piece(dx, dy):
        return g_sent.at[DY.index(dy), dx * PIECE : (dx + 1) * PIECE]

    def gx_copy(dx, dy):
        return remote(g_piece(dx, dy), gx_in.at[dx - 1, dy], "gx", (dx - 1, dy), x_peer[dx])

    def grad_block(k):
        half_swap(k, 1, other).wait_recv()
        rows = slice(k * BLOCK, (k + 1) * BLOCK)
        g[k] = nt(ah[0, 1, rows, :], w_full[:, 0:HALF]) + nt(
            ah[1, 1, rows, :], w_full[:, HALF:HIDDEN]
        )
        g_sent[k] = g[k].astype(BF16)
        for dx in (2, 1, 3):
            start(gx_copy(dx, DY[k]))

    def x_sum(dy):
        total = g[DY.index(dy), 0:PIECE]
        for dx in range(1, NX):
            gx_copy(dx, dy).wait_recv()
            total = total + gx_in[dx - 1, dy].astype(F32)
        return total

    def gy_copy(dy):
        if dy == 2:
            return remote(gy_far.at[0], gy_far.at[1], "gy", (dy - 1,), y_peer[dy])
        return remote(gy_out.at[dy - 1], gy_in.at[dy - 1], "gy", (dy - 1,), y_peer[dy])

    def y_part(dy):
        total = x_sum(dy)
        if dy == 2:
            gy_far[0] = total.astype(BF16)
        else:
            gy_out[dy - 1] = total
        start(gy_copy(dy))

    def weight_grads(a):
        for half in range(2):
            cols = slice(half * HALF, (half + 1) * HALF)
            if a == 1:
                grad_w_in[:, cols] = tn(panel[0, :, 0:WIDTH], ah[half, 1]).astype(BF16)
                continue
            if half == 0:
                for k in range(4):
                    half_swap(k, 0, other).wait_recv()
            grad_w_out[cols, :] = tn(ah[half, 0], panel[1, :, 0:WIDTH]).astype(BF16)

    for a in range(2):
        own[a].wait()
        for d in (1, 3):
            start(y_copy(d, a))
        own_ready(0, a)
    own[4].wait()
    own[5].wait()
    w_swap = [
        remote(w_full.at[:, other_cols], wi.at[WIDTH : 2 * WIDTH, :], "wx", (0,), twin),
        remote(wo_other, wo.at[:, WIDTH : 2 * WIDTH], "wx", (1,), twin),
    ]
    for copy in w_swap:
        start(copy)
    own[2].wait()
    own[3].wait()
    y_arrive(3, 0)
    x_arrive(0, 0)
    y_arrive(1, 0)
    x_arrive(0, 1)
    y_arrive(1, 1)
    for copy in w_swap:
        copy.wait_recv()
    matmuls(0, 0)
    rs_step(0, 0, 0)
    rs_step(0, 1, 0)
    y_arrive(3, 1)
    matmuls(0, 1)
    rs_step(0, 0, 1)
    rs_step(0, 1, 1)
    x_arrive(1, 0)
    y_arrive(2, 0)
    x_arrive(3, 0)
    matmuls(1, 0)
    rs_step(1, 0, 0)
    rs_step(1, 1, 0)
    rs_step(0, 2, 0)
    y_arrive(2, 1)
    x_arrive(3, 1)
    matmuls(2, 0)
    rs_step(2, 0, 0)
    rs_step(2, 1, 0)
    rs_step(0, 2, 1)
    x_arrive(1, 1)
    matmuls(2, 1)
    rs_step(2, 0, 1)
    rs_step(2, 1, 1)
    matmuls(1, 1)
    rs_step(1, 0, 1)
    rs_step(1, 1, 1)
    x_arrive(2, 0)
    matmuls(3, 0)
    rs_step(0, 3, 0)
    rs_step(3, 0, 0)
    rs_step(1, 2, 0)
    rs_step(3, 1, 0)
    x_arrive(2, 1)
    matmuls(3, 1)
    rs_step(0, 3, 1)
    rs_step(2, 2, 0)
    rs_step(3, 0, 1)
    rs_step(2, 2, 1)
    rs_step(3, 1, 1)
    rs_step(1, 2, 1)
    rs_end(0, 0)
    rs_step(1, 3, 0)
    rs_step(3, 2, 0)
    rs_end(0, 1)
    rs_step(2, 3, 0)
    rs_step(2, 3, 1)
    rs_step(3, 2, 1)
    rs_step(1, 3, 1)
    rs_end(1, 0)
    rs_step(3, 3, 0)
    gelu(0)
    rs_end(2, 0)
    rs_end(2, 1)
    rs_step(3, 3, 1)
    rs_end(1, 1)
    rs_end(3, 0)
    ag_step(0, 1, 1)
    ag_step(0, 1, 0)
    rs_end(3, 1)
    gelu(2)
    gelu(1)
    ag_step(0, 2, 1)
    ag_step(0, 2, 0)
    ag_step(2, 1, 1)
    gelu(3)
    ag_step(2, 1, 0)
    ag_step(1, 1, 1)
    ag_step(1, 1, 0)
    ag_end(0, 1)
    ag_step(2, 2, 1)
    ag_end(0, 0)
    ag_step(3, 1, 1)
    grad_block(0)
    ag_step(3, 1, 0)
    ag_step(2, 2, 0)
    ag_step(1, 2, 1)
    ag_step(1, 2, 0)
    ag_step(3, 2, 1)
    ag_end(2, 1)
    ag_step(3, 2, 0)
    grad_block(2)
    ag_end(2, 0)
    ag_end(1, 1)
    ag_end(1, 0)
    grad_block(1)
    ag_end(3, 1)
    y_part(3)
    ag_end(3, 0)
    grad_block(3)
    weight_grads(1)
    weight_grads(0)
    y_part(1)
    y_part(2)
    total = x_sum(0)
    for dy in range(1, NYH):
        gy_copy(dy).wait_recv()
        total = total + (gy_far[1].astype(F32) if dy == 2 else gy_in[dy - 1])
    grad_inputs[...] = total.astype(BF16)

    for copy in sent:
        copy.wait_send()


def store(*refs):
    half = len(refs) // 2
    sems = refs[-1]
    copies = [
        pltpu.make_async_copy(refs[i], refs[half + i], sems.at[i]) for i in range(half)
    ]
    for copy in copies:
        copy.start()
    for copy in copies:
        copy.wait()


def body(inputs, out_grad, w_in, w_out):
    hbm = pl.BlockSpec(memory_space=pltpu.HBM)
    vmem = pl.BlockSpec(memory_space=pltpu.VMEM)
    dma = pltpu.SemaphoreType.DMA
    shapes = ((PIECE, WIDTH), (WIDTH, HIDDEN), (HIDDEN, WIDTH))
    results = pl.pallas_call(
        kernel,
        out_shape=tuple(pltpu.VMEM(shape, BF16) for shape in shapes),
        in_specs=[hbm] * 4,
        out_specs=(vmem,) * 3,
        scratch_shapes=[
            pltpu.VMEM((2, TOKENS, 2 * WIDTH), BF16),
            pltpu.VMEM((2 * WIDTH, HALF), BF16),
            pltpu.VMEM((HALF, 2 * WIDTH), BF16),
            pltpu.VMEM((WIDTH, HIDDEN), BF16),
            pltpu.VMEM((HALF, WIDTH), BF16),
            pltpu.VMEM((4, 2, BLOCK, HALF), F32),
            pltpu.VMEM((2, 4, 4, 2, CHUNK, HALF), BF16),
            pltpu.VMEM((2, 4, 4, 2, CHUNK, HALF), BF16),
            pltpu.VMEM((4, 2, CHUNK, HALF), F32),
            pltpu.VMEM((4, 2, CHUNK, HALF), F32),
            pltpu.VMEM((2, 2, TOKENS, HALF), BF16),
            pltpu.VMEM((4, BLOCK, WIDTH), F32),
            pltpu.VMEM((3, 4, PIECE, WIDTH), BF16),
            pltpu.VMEM((3, PIECE, WIDTH), F32),
            pltpu.VMEM((3, PIECE, WIDTH), F32),
            pltpu.VMEM((4, BLOCK, WIDTH), BF16),
            pltpu.VMEM((2, PIECE, WIDTH), BF16),
            dma((6,)),
            *(dma(shape) for shape in SEMAPHORES.values() for _ in range(2)),
        ],
        compiler_params=pltpu.CompilerParams(
            collective_id=0, has_side_effects=True, vmem_limit_bytes=60 << 20
        ),
        cost_estimate=pl.CostEstimate(
            flops=6 * 10**9, bytes_accessed=5 * 10**6, transcendentals=10**6
        ),
        name="ffn_backward",
    )(inputs, out_grad, w_in, w_out)
    return pl.pallas_call(
        store,
        out_shape=tuple(jax.ShapeDtypeStruct(shape, BF16) for shape in shapes),
        in_specs=[pl.BlockSpec(memory_space=pl.ANY)] * 3,
        out_specs=(pl.BlockSpec(memory_space=pl.ANY),) * 3,
        scratch_shapes=[dma((3,))],
        compiler_params=pltpu.CompilerParams(vmem_limit_bytes=1 << 20),
        name="store_results",
    )(*results)


def solution(mesh):
    return jax.shard_map(
        body,
        mesh=mesh,
        in_specs=(P("col", "row"), P("col", "row"), P("row", "col"), P("col", "row")),
        out_specs=(P("col", "row"), P("row", "col"), P("col", "row")),
        check_vma=False,
    )
```

time: 82 us -> 77.1 us (0.940)
  the two profiles are of different devices: /device:TPU:9 before, /device:TPU:1 now
where the time goes in v3:
time: 77.1 us; the launch traced here: 76.6 us
  Pallas kernels  76 us (99%)
    pallas_call x1, Pallas kernels, body(): pl.pallas_call(kernel, out_shape=tuple((pltpu.VMEM(shape, BF16) for shape...  74.6 us

profile of v3, /device:TPU:1, one launch (start us, length us, event | category | flops | bytes accessed | tf_op | source)
XLA Modules:
  0.0 76.6 jit_solution(2883062668739623394)
XLA Ops:
  0.6 74.6 %ffn_backward.1 = (bf16[32,384]{1,0:T(8,128)(2,1)S(1)}, bf16[384,1536]{1,0:T(8,128)(2,1)S(1)}, bf16[1536,384]{1,0:T(8,128)(2,1)S(1)}) custom-call(bf16[32,384]{1,0:T(8,128)(2,1)} %inputs.1, bf16[32,384]{1,0:T(8,128)(2,1)} %out_grad.1, bf16[384,1536]{1,0:T(8,128)(2,1)} %w_in.1, bf16[1536,384]{1,0:T(8,128)(2,1)} %w_out.1), custom_call_target="tpu_custom_call" | custom-call | flops 6000000000 | bytes 5000000 | tf_op jit(solution)/shard_map/ffn_backward/pallas_call | solution.py:426
  75.2 1.4 %store_results.1 = (bf16[32,384]{1,0:T(8,128)(2,1)}, bf16[384,1536]{1,0:T(8,128)(2,1)}, bf16[1536,384]{1,0:T(8,128)(2,1)}) custom-call(bf16[32,384]{1,0:T(8,128)(2,1)S(1)} %get-tuple-element.6.refs_0_, bf16[384,1536]{1,0:T(8,128)(2,1)S(1)} %get-tuple-element.7.refs_1_, bf16[1536,384]{1,0:T(8,128)(2,1)S(1)} %get-tuple-element.8.refs_2_), custom_call_target="tpu_custom_call" | custom-call | tf_op jit(solution)/shard_map/store_results/pallas_call | solution.py:460

commit v4 on v3

--- a/solution.py
+++ b/solution.py
@@ -22,6 +22,7 @@
 WIDTH = 384
 HIDDEN = 1536
 HALF = HIDDEN // 2
+SUB = HALF // 2
 
 DY = (0, 1, 3, 2)
 
@@ -31,9 +32,12 @@
     "ys": (2, 2),
     "yf": (2,),
     "xs": (2, 3, 4),
-    "rs": (2, 4, 4, 2),
-    "ye": (4, 2),
+    "rs": (2, 4, 3, 2),
+    "rl": (2, 2, 4, 2),
+    "rp": (4, 2),
     "ag": (2, 4, 4, 2),
+    "ac": (2, 4, 2),
+    "ap": (4, 2),
     "cf": (4, 2),
     "gx": (3, 4),
     "gy": (3,),
@@ -65,7 +69,7 @@
 def kernel(
     inputs, out_grad, w_in, w_out,
     grad_inputs, grad_w_in, grad_w_out,
-    panel, wi, wo, w_full, wo_other, part, rs_out, rs_in, y_out, y_in, ah,
+    panel, wi, wo, w_full, wo_other, part, rs_out, rs_in, rs_last, rp_out, rp_in, ah,
     g, gx_in, gy_out, gy_in, g_sent, gy_far, local_sem, *pairs,
 ):
     row, col = lax.axis_index("row"), lax.axis_index("col")
@@ -79,6 +83,7 @@
     twin = device(core=other)
     partner = device(y_lo=1 - y_lo)
     z_next = (device(z=(z + 1) % NZ), device(z=(z + NZ - 1) % NZ))
+    z_cross = tuple(device(z=(z + d) % NZ, y_lo=1 - y_lo) for d in (1, NZ - 1))
     z_over = (device(z=(z + 2) % NZ), device(z=(z + NZ - 2) % NZ))
     x_peer = [None, *(device(x=(x + d) % NX) for d in range(1, NX))]
     y_peer = [None, *(device(y_hi=(y_hi + d) % NYH) for d in range(1, NYH))]
@@ -98,6 +103,8 @@
         sent.append(copy)
 
     half_cols = pl.ds(pl.multiple_of(core * HALF, 128), HALF)
+    sub = pl.ds(pl.multiple_of(y_lo * SUB, 128), SUB)
+    other_sub = pl.ds(pl.multiple_of((1 - y_lo) * SUB, 128), SUB)
     other_cols = pl.ds(pl.multiple_of(other * HALF, 128), HALF)
     own = [
         pltpu.make_async_copy(inputs, panel.at[0, 0:PIECE, 0:WIDTH], local_sem.at[0]),
@@ -111,7 +118,7 @@
         copy.start()
 
     barrier = pltpu.get_barrier_semaphore()
-    greeted = [twin, partner, *z_next, *z_over, *x_peer[1:], *y_peer[1:]]
+    greeted = [twin, partner, *z_next, *z_cross, *z_over, *x_peer[1:], *y_peer[1:]]
     for peer in greeted:
         pl.semaphore_signal(barrier, inc=1, device_id=peer, device_id_type=MESH)
     pl.semaphore_wait(barrier, len(greeted))
@@ -173,6 +180,16 @@
         return remote(
             rs_out.at[way, k, s, a], rs_in.at[way, k, s, a], "rs", (way, k, s, a), to
         )
+
+    def rl_copy(way, cross, k, a):
+        return remote(
+            rs_out.at[way, k, 3, a, :, other_sub if cross else sub],
+            rs_last.at[way, cross, k, a], "rl", (way, cross, k, a),
+            z_cross[way] if cross else z_next[way],
+        )
+
+    def rp_copy(k, a):
+        return remote(rp_out.at[k, a], rp_in.at[k, a], "rp", (k, a), partner)
 
     def rs_step(k, s, a):
         for way in range(2):
@@ -184,43 +201,62 @@
                 rs_copy(way, k, earlier, a).wait_recv()
                 term = term + rs_in[way, k, earlier, a].astype(F32)
             rs_out[way, k, s, a] = term.astype(BF16)
-            start(rs_copy(way, k, s, a))
-
-    def y_exchange(k, a):
-        return remote(y_out.at[k, a], y_in.at[k, a], "ye", (k, a), partner)
-
-    def rs_end(k, a):
-        for way in range(2):
-            rs_copy(way, k, 3, a).wait_recv()
-        y_out[k, a] = part[k, a, chunk(z * CHUNK), :] + (
-            rs_in[0, k, 3, a].astype(F32) + rs_in[1, k, 3, a].astype(F32)
-        )
-        start(y_exchange(k, a))
+            if s < 3:
+                start(rs_copy(way, k, s, a))
+            else:
+                start(rl_copy(way, 1, k, a))
+                start(rl_copy(way, 0, k, a))
+        if s == 0:
+            rp_out[k, a] = part[k, a, chunk(z * CHUNK), other_sub].astype(BF16)
+            start(rp_copy(k, a))
 
     def ag_copy(way, k, s, a, origin):
-        ref = ah.at[core, a, chunk(k * BLOCK + origin * CHUNK), :]
+        rows = chunk(k * BLOCK + origin * CHUNK)
+        ref = ah.at[core, a, rows, sub] if s == 0 else ah.at[core, a, rows, :]
         to = z_over[way] if s == 3 else z_next[way]
         return remote(ref, ref, "ag", (way, k, s, a), to)
 
+    def ag_cross(way, k, a, origin, cols):
+        ref = ah.at[core, a, chunk(k * BLOCK + origin * CHUNK), cols]
+        return remote(ref, ref, "ac", (way, k, a), z_cross[way])
+
+    def ag_partner(k, a, cols):
+        ref = ah.at[core, a, chunk(k * BLOCK + z * CHUNK), cols]
+        return remote(ref, ref, "ap", (k, a), partner)
+
     def ag_origin(way, s):
         return (z + NZ + (-s if way == 0 else s)) % NZ
 
     def ag_step(k, s, a):
         for way in range(2):
-            if s > 0:
-                ag_copy(way, k, s - 1, a, ag_origin(way, s)).wait_recv()
-            start(ag_copy(way, k, s, a, ag_origin(way, s)))
+            origin = ag_origin(way, s)
+            if s == 0:
+                start(ag_cross(way, k, a, origin, sub))
+            else:
+                ag_copy(way, k, s - 1, a, origin).wait_recv()
+            if s == 1:
+                ag_cross(way, k, a, origin, other_sub).wait_recv()
+            start(ag_copy(way, k, s, a, origin))
             if s == 2 and way == a:
-                start(ag_copy(way, k, 3, a, ag_origin(way, 2)))
+                start(ag_copy(way, k, 3, a, origin))
+        if s == 0:
+            start(ag_partner(k, a, sub))
 
     def gelu(k):
+        sums = []
         for a in range(2):
-            y_exchange(k, a).wait_recv()
-        value, grad = activate(y_out[k, 0] + y_in[k, 0], y_out[k, 1] + y_in[k, 1])
+            rp_copy(k, a).wait_recv()
+            total = part[k, a, chunk(z * CHUNK), sub] + rp_in[k, a].astype(F32)
+            for way in range(2):
+                for cross in range(2):
+                    rl_copy(way, cross, k, a).wait_recv()
+                    total = total + rs_last[way, cross, k, a].astype(F32)
+            sums.append(total)
+        value, grad = activate(*sums)
         rows = chunk(k * BLOCK + z * CHUNK)
-        ah[core, 1, rows, :] = grad
+        ah[core, 1, rows, sub] = grad
         ag_step(k, 0, 1)
-        ah[core, 0, rows, :] = value
+        ah[core, 0, rows, sub] = value
         ag_step(k, 0, 0)
 
     def half_swap(k, a, half):
@@ -231,6 +267,7 @@
         for way in range(2):
             ag_copy(way, k, 2, a, ag_origin(way, 3)).wait_recv()
         ag_copy(a, k, 3, a, ag_origin(a, 4)).wait_recv()
+        ag_partner(k, a, other_sub).wait_recv()
         start(half_swap(k, a, core))
 
     def g_piece(dx, dy):
@@ -295,32 +332,32 @@
         start(copy)
     own[2].wait()
     own[3].wait()
+    y_arrive(1, 0)
     y_arrive(3, 0)
     x_arrive(0, 0)
-    y_arrive(1, 0)
+    y_arrive(1, 1)
     x_arrive(0, 1)
-    y_arrive(1, 1)
+    y_arrive(3, 1)
     for copy in w_swap:
         copy.wait_recv()
     matmuls(0, 0)
     rs_step(0, 0, 0)
     rs_step(0, 1, 0)
-    y_arrive(3, 1)
     matmuls(0, 1)
     rs_step(0, 0, 1)
     rs_step(0, 1, 1)
+    x_arrive(3, 0)
+    y_arrive(2, 0)
     x_arrive(1, 0)
-    y_arrive(2, 0)
-    x_arrive(3, 0)
+    matmuls(2, 0)
+    rs_step(2, 0, 0)
+    rs_step(2, 1, 0)
+    rs_step(0, 2, 0)
+    y_arrive(2, 1)
+    x_arrive(3, 1)
     matmuls(1, 0)
     rs_step(1, 0, 0)
     rs_step(1, 1, 0)
-    rs_step(0, 2, 0)
-    y_arrive(2, 1)
-    x_arrive(3, 1)
-    matmuls(2, 0)
-    rs_step(2, 0, 0)
-    rs_step(2, 1, 0)
     rs_step(0, 2, 1)
     x_arrive(1, 1)
     matmuls(2, 1)
@@ -330,55 +367,47 @@
     rs_step(1, 0, 1)
     rs_step(1, 1, 1)
     x_arrive(2, 0)
+    rs_step(2, 2, 0)
     matmuls(3, 0)
     rs_step(0, 3, 0)
     rs_step(3, 0, 0)
-    rs_step(1, 2, 0)
     rs_step(3, 1, 0)
     x_arrive(2, 1)
+    rs_step(1, 2, 0)
     matmuls(3, 1)
+    rs_step(3, 0, 1)
+    rs_step(3, 1, 1)
+    rs_step(2, 2, 1)
     rs_step(0, 3, 1)
-    rs_step(2, 2, 0)
-    rs_step(3, 0, 1)
-    rs_step(2, 2, 1)
-    rs_step(3, 1, 1)
     rs_step(1, 2, 1)
-    rs_end(0, 0)
+    rs_step(2, 3, 0)
+    rs_step(3, 2, 0)
     rs_step(1, 3, 0)
-    rs_step(3, 2, 0)
-    rs_end(0, 1)
-    rs_step(2, 3, 0)
+    rs_step(3, 2, 1)
     rs_step(2, 3, 1)
-    rs_step(3, 2, 1)
+    gelu(0)
     rs_step(1, 3, 1)
-    rs_end(1, 0)
     rs_step(3, 3, 0)
-    gelu(0)
-    rs_end(2, 0)
-    rs_end(2, 1)
     rs_step(3, 3, 1)
-    rs_end(1, 1)
-    rs_end(3, 0)
+    gelu(2)
     ag_step(0, 1, 1)
     ag_step(0, 1, 0)
-    rs_end(3, 1)
-    gelu(2)
     gelu(1)
+    gelu(3)
+    ag_step(2, 1, 1)
     ag_step(0, 2, 1)
+    ag_step(2, 1, 0)
     ag_step(0, 2, 0)
-    ag_step(2, 1, 1)
-    gelu(3)
-    ag_step(2, 1, 0)
     ag_step(1, 1, 1)
     ag_step(1, 1, 0)
-    ag_end(0, 1)
     ag_step(2, 2, 1)
-    ag_end(0, 0)
     ag_step(3, 1, 1)
-    grad_block(0)
     ag_step(3, 1, 0)
     ag_step(2, 2, 0)
+    ag_end(0, 1)
     ag_step(1, 2, 1)
+    ag_end(0, 0)
+    grad_block(0)
     ag_step(1, 2, 0)
     ag_step(3, 2, 1)
     ag_end(2, 1)
@@ -389,8 +418,8 @@
     ag_end(1, 0)
     grad_block(1)
     ag_end(3, 1)
+    ag_end(3, 0)
     y_part(3)
-    ag_end(3, 0)
     grad_block(3)
     weight_grads(1)
     weight_grads(0)
@@ -437,8 +466,9 @@
             pltpu.VMEM((4, 2, BLOCK, HALF), F32),
             pltpu.VMEM((2, 4, 4, 2, CHUNK, HALF), BF16),
             pltpu.VMEM((2, 4, 4, 2, CHUNK, HALF), BF16),
-            pltpu.VMEM((4, 2, CHUNK, HALF), F32),
-            pltpu.VMEM((4, 2, CHUNK, HALF), F32),
+            pltpu.VMEM((2, 2, 4, 2, CHUNK, SUB), BF16),
+            pltpu.VMEM((4, 2, CHUNK, SUB), BF16),
+            pltpu.VMEM((4, 2, CHUNK, SUB), BF16),
             pltpu.VMEM((2, 2, TOKENS, HALF), BF16),
             pltpu.VMEM((4, BLOCK, WIDTH), F32),
             pltpu.VMEM((3, 4, PIECE, WIDTH), BF16),

time: 77.1 us -> 74.9 us (0.971)
  Pallas kernels: 76 us -> 73.8 us
    pallas_call x1, Pallas kernels: 74.6 us -> 72.4 us  [body(): pl.pallas_call(kernel, out_shape=tuple((pltpu.VMEM(shape, BF16) for shape...]
where the time goes in v4:
time: 74.9 us; the launch traced here: 74.5 us
  Pallas kernels  73.8 us (99%)
    pallas_call x1, Pallas kernels, body(): pl.pallas_call(kernel, out_shape=tuple((pltpu.VMEM(shape, BF16) for shape...  72.4 us

profile of v4, /device:TPU:1, one launch (start us, length us, event | category | flops | bytes accessed | tf_op | source)
XLA Modules:
  0.0 74.5 jit_solution(7055744670388532792)
XLA Ops:
  0.6 72.4 %ffn_backward.1 = (bf16[32,384]{1,0:T(8,128)(2,1)S(1)}, bf16[384,1536]{1,0:T(8,128)(2,1)S(1)}, bf16[1536,384]{1,0:T(8,128)(2,1)S(1)}) custom-call(bf16[32,384]{1,0:T(8,128)(2,1)} %inputs.1, bf16[32,384]{1,0:T(8,128)(2,1)} %out_grad.1, bf16[384,1536]{1,0:T(8,128)(2,1)} %w_in.1, bf16[1536,384]{1,0:T(8,128)(2,1)} %w_out.1), custom_call_target="tpu_custom_call" | custom-call | flops 6000000000 | bytes 5000000 | tf_op jit(solution)/shard_map/ffn_backward/pallas_call | solution.py:455
  73.0 1.4 %store_results.1 = (bf16[32,384]{1,0:T(8,128)(2,1)}, bf16[384,1536]{1,0:T(8,128)(2,1)}, bf16[1536,384]{1,0:T(8,128)(2,1)}) custom-call(bf16[32,384]{1,0:T(8,128)(2,1)S(1)} %get-tuple-element.6.refs_0_, bf16[384,1536]{1,0:T(8,128)(2,1)S(1)} %get-tuple-element.7.refs_1_, bf16[1536,384]{1,0:T(8,128)(2,1)S(1)} %get-tuple-element.8.refs_2_), custom_call_target="tpu_custom_call" | custom-call | tf_op jit(solution)/shard_map/store_results/pallas_call | solution.py:490

commit v5 on v4

--- a/solution.py
+++ b/solution.py
@@ -36,8 +36,9 @@
     "rl": (2, 2, 4, 2),
     "rp": (4, 2),
     "ag": (2, 4, 4, 2),
-    "ac": (2, 4, 2),
-    "ap": (4, 2),
+    "ac": (2, 4),
+    "ap": (4,),
+    "aq": (4,),
     "cf": (4, 2),
     "gx": (3, 4),
     "gy": (3,),
@@ -212,17 +213,21 @@
 
     def ag_copy(way, k, s, a, origin):
         rows = chunk(k * BLOCK + origin * CHUNK)
-        ref = ah.at[core, a, rows, sub] if s == 0 else ah.at[core, a, rows, :]
+        ref = ah.at[core, a, rows, sub] if s == 0 or a == 0 else ah.at[core, a, rows, :]
         to = z_over[way] if s == 3 else z_next[way]
         return remote(ref, ref, "ag", (way, k, s, a), to)
 
-    def ag_cross(way, k, a, origin, cols):
-        ref = ah.at[core, a, chunk(k * BLOCK + origin * CHUNK), cols]
-        return remote(ref, ref, "ac", (way, k, a), z_cross[way])
-
-    def ag_partner(k, a, cols):
-        ref = ah.at[core, a, chunk(k * BLOCK + z * CHUNK), cols]
-        return remote(ref, ref, "ap", (k, a), partner)
+    def ag_cross(way, k, origin, cols):
+        ref = ah.at[core, 1, chunk(k * BLOCK + origin * CHUNK), cols]
+        return remote(ref, ref, "ac", (way, k), z_cross[way])
+
+    def ag_partner(k, cols):
+        ref = ah.at[core, 1, chunk(k * BLOCK + z * CHUNK), cols]
+        return remote(ref, ref, "ap", (k,), partner)
+
+    def act_swap(k, cols):
+        ref = ah.at[core, 0, k * BLOCK : (k + 1) * BLOCK, cols]
+        return remote(ref, ref, "aq", (k,), partner)
 
     def ag_origin(way, s):
         return (z + NZ + (-s if way == 0 else s)) % NZ
@@ -230,17 +235,17 @@
     def ag_step(k, s, a):
         for way in range(2):
             origin = ag_origin(way, s)
-            if s == 0:
-                start(ag_cross(way, k, a, origin, sub))
-            else:
+            if s == 0 and a == 1:
+                start(ag_cross(way, k, origin, sub))
+            if s > 0:
                 ag_copy(way, k, s - 1, a, origin).wait_recv()
-            if s == 1:
-                ag_cross(way, k, a, origin, other_sub).wait_recv()
+            if s == 1 and a == 1:
+                ag_cross(way, k, origin, other_sub).wait_recv()
             start(ag_copy(way, k, s, a, origin))
             if s == 2 and way == a:
                 start(ag_copy(way, k, 3, a, origin))
-        if s == 0:
-            start(ag_partner(k, a, sub))
+        if s == 0 and a == 1:
+            start(ag_partner(k, sub))
 
     def gelu(k):
         sums = []
@@ -267,8 +272,15 @@
         for way in range(2):
             ag_copy(way, k, 2, a, ag_origin(way, 3)).wait_recv()
         ag_copy(a, k, 3, a, ag_origin(a, 4)).wait_recv()
-        ag_partner(k, a, other_sub).wait_recv()
-        start(half_swap(k, a, core))
+        if a == 0:
+            start(act_swap(k, sub))
+        else:
+            ag_partner(k, other_sub).wait_recv()
+            start(half_swap(k, 1, core))
+
+    def act_end(k):
+        act_swap(k, other_sub).wait_recv()
+        start(half_swap(k, 0, core))
 
     def g_piece(dx, dy):
         return g_sent.at[DY.index(dy), dx * PIECE : (dx + 1) * PIECE]
@@ -332,12 +344,12 @@
         start(copy)
     own[2].wait()
     own[3].wait()
-    y_arrive(1, 0)
     y_arrive(3, 0)
     x_arrive(0, 0)
+    y_arrive(1, 0)
+    y_arrive(3, 1)
     y_arrive(1, 1)
     x_arrive(0, 1)
-    y_arrive(3, 1)
     for copy in w_swap:
         copy.wait_recv()
     matmuls(0, 0)
@@ -346,84 +358,88 @@
     matmuls(0, 1)
     rs_step(0, 0, 1)
     rs_step(0, 1, 1)
+    x_arrive(1, 0)
+    y_arrive(2, 0)
     x_arrive(3, 0)
-    y_arrive(2, 0)
-    x_arrive(1, 0)
+    matmuls(1, 0)
+    y_arrive(2, 1)
+    rs_step(1, 0, 0)
+    rs_step(0, 2, 0)
+    rs_step(1, 1, 0)
+    x_arrive(1, 1)
     matmuls(2, 0)
     rs_step(2, 0, 0)
     rs_step(2, 1, 0)
-    rs_step(0, 2, 0)
-    y_arrive(2, 1)
     x_arrive(3, 1)
-    matmuls(1, 0)
-    rs_step(1, 0, 0)
-    rs_step(1, 1, 0)
+    matmuls(1, 1)
+    rs_step(1, 0, 1)
+    rs_step(1, 1, 1)
     rs_step(0, 2, 1)
-    x_arrive(1, 1)
     matmuls(2, 1)
     rs_step(2, 0, 1)
     rs_step(2, 1, 1)
-    matmuls(1, 1)
-    rs_step(1, 0, 1)
-    rs_step(1, 1, 1)
     x_arrive(2, 0)
-    rs_step(2, 2, 0)
     matmuls(3, 0)
+    rs_step(3, 0, 0)
     rs_step(0, 3, 0)
-    rs_step(3, 0, 0)
-    rs_step(3, 1, 0)
     x_arrive(2, 1)
     rs_step(1, 2, 0)
+    rs_step(3, 1, 0)
     matmuls(3, 1)
     rs_step(3, 0, 1)
     rs_step(3, 1, 1)
+    rs_step(1, 2, 1)
+    rs_step(2, 2, 0)
+    rs_step(0, 3, 1)
     rs_step(2, 2, 1)
-    rs_step(0, 3, 1)
-    rs_step(1, 2, 1)
+    rs_step(1, 3, 0)
+    rs_step(3, 2, 0)
+    rs_step(3, 2, 1)
+    rs_step(1, 3, 1)
     rs_step(2, 3, 0)
-    rs_step(3, 2, 0)
-    rs_step(1, 3, 0)
-    rs_step(3, 2, 1)
+    gelu(0)
     rs_step(2, 3, 1)
-    gelu(0)
-    rs_step(1, 3, 1)
     rs_step(3, 3, 0)
     rs_step(3, 3, 1)
+    gelu(1)
+    ag_step(0, 1, 0)
+    ag_step(0, 1, 1)
     gelu(2)
-    ag_step(0, 1, 1)
-    ag_step(0, 1, 0)
-    gelu(1)
     gelu(3)
-    ag_step(2, 1, 1)
+    ag_step(1, 1, 0)
+    ag_step(1, 1, 1)
+    ag_step(0, 2, 0)
     ag_step(0, 2, 1)
     ag_step(2, 1, 0)
-    ag_step(0, 2, 0)
-    ag_step(1, 1, 1)
-    ag_step(1, 1, 0)
-    ag_step(2, 2, 1)
+    ag_step(2, 1, 1)
+    ag_step(3, 1, 0)
+    ag_step(1, 2, 0)
     ag_step(3, 1, 1)
-    ag_step(3, 1, 0)
+    ag_step(1, 2, 1)
+    ag_end(0, 0)
     ag_step(2, 2, 0)
     ag_end(0, 1)
-    ag_step(1, 2, 1)
-    ag_end(0, 0)
+    ag_step(2, 2, 1)
+    ag_step(3, 2, 0)
     grad_block(0)
-    ag_step(1, 2, 0)
+    ag_end(1, 0)
     ag_step(3, 2, 1)
+    ag_end(1, 1)
+    ag_end(2, 0)
+    act_end(0)
+    grad_block(1)
     ag_end(2, 1)
-    ag_step(3, 2, 0)
+    ag_end(3, 0)
     grad_block(2)
-    ag_end(2, 0)
-    ag_end(1, 1)
-    ag_end(1, 0)
-    grad_block(1)
     ag_end(3, 1)
-    ag_end(3, 0)
-    y_part(3)
+    act_end(1)
     grad_block(3)
     weight_grads(1)
+    y_part(1)
+    act_end(2)
+    act_end(3)
+    y_part(3)
     weight_grads(0)
-    y_part(1)
     y_part(2)
     total = x_sum(0)
     for dy in range(1, NYH):

time: 74.9 us -> 73.8 us (0.985)
  Pallas kernels: 73.8 us -> 72.7 us
    pallas_call x1, Pallas kernels: 72.4 us -> 71.3 us  [body(): pl.pallas_call(kernel, out_shape=tuple((pltpu.VMEM(shape, BF16) for shape...]
where the time goes in v5:
time: 73.8 us; the launch traced here: 73.4 us
  Pallas kernels  72.7 us (99%)
    pallas_call x1, Pallas kernels, body(): pl.pallas_call(kernel, out_shape=tuple((pltpu.VMEM(shape, BF16) for shape...  71.3 us

profile of v5, /device:TPU:1, one launch (start us, length us, event | category | flops | bytes accessed | tf_op | source)
XLA Modules:
  0.0 73.4 jit_solution(5149352166363712251)
XLA Ops:
  0.6 71.3 %ffn_backward.1 = (bf16[32,384]{1,0:T(8,128)(2,1)S(1)}, bf16[384,1536]{1,0:T(8,128)(2,1)S(1)}, bf16[1536,384]{1,0:T(8,128)(2,1)S(1)}) custom-call(bf16[32,384]{1,0:T(8,128)(2,1)} %inputs.1, bf16[32,384]{1,0:T(8,128)(2,1)} %out_grad.1, bf16[384,1536]{1,0:T(8,128)(2,1)} %w_in.1, bf16[1536,384]{1,0:T(8,128)(2,1)} %w_out.1), custom_call_target="tpu_custom_call" | custom-call | flops 6000000000 | bytes 5000000 | tf_op jit(solution)/shard_map/ffn_backward/pallas_call | solution.py:471
  71.9 1.4 %store_results.1 = (bf16[32,384]{1,0:T(8,128)(2,1)}, bf16[384,1536]{1,0:T(8,128)(2,1)}, bf16[1536,384]{1,0:T(8,128)(2,1)}) custom-call(bf16[32,384]{1,0:T(8,128)(2,1)S(1)} %get-tuple-element.6.refs_0_, bf16[384,1536]{1,0:T(8,128)(2,1)S(1)} %get-tuple-element.7.refs_1_, bf16[1536,384]{1,0:T(8,128)(2,1)S(1)} %get-tuple-element.8.refs_2_), custom_call_target="tpu_custom_call" | custom-call | tf_op jit(solution)/shard_map/store_results/pallas_call | solution.py:506

commit v6 on v5

--- a/solution.py
+++ b/solution.py
@@ -25,6 +25,8 @@
 SUB = HALF // 2
 
 DY = (0, 1, 3, 2)
+
+STORES = 4
 
 SEMAPHORES = {
     "core": (2, 4, 4),
@@ -454,9 +456,15 @@
 def store(*refs):
     half = len(refs) // 2
     sems = refs[-1]
-    copies = [
-        pltpu.make_async_copy(refs[i], refs[half + i], sems.at[i]) for i in range(half)
-    ]
+    copies = []
+    for i in range(half):
+        rows = refs[i].shape[0]
+        step = rows if i == 0 else rows // STORES
+        for j in range(rows // step):
+            part = slice(j * step, (j + 1) * step)
+            copies.append(
+                pltpu.make_async_copy(refs[i].at[part], refs[half + i].at[part], sems.at[i, j])
+            )
     for copy in copies:
         copy.start()
     for copy in copies:
@@ -508,7 +516,7 @@
         out_shape=tuple(jax.ShapeDtypeStruct(shape, BF16) for shape in shapes),
         in_specs=[pl.BlockSpec(memory_space=pl.ANY)] * 3,
         out_specs=(pl.BlockSpec(memory_space=pl.ANY),) * 3,
-        scratch_shapes=[dma((3,))],
+        scratch_shapes=[dma((3, STORES))],
         compiler_params=pltpu.CompilerParams(vmem_limit_bytes=1 << 20),
         name="store_results",
     )(*results)

time: 73.8 us -> 73.9 us (level)
  no operation moved by 1% of the time
where the time goes in v6:
time: 73.9 us; the launch traced here: 73.5 us
  Pallas kernels  72.8 us (99%)
    pallas_call x1, Pallas kernels, body(): pl.pallas_call(kernel, out_shape=tuple((pltpu.VMEM(shape, BF16) for shape...  71.3 us
    pallas_call x1, Pallas kernels, body(): pl.pallas_call(store, out_shape=tuple((jax.ShapeDtypeStruct(shape, BF16)...  1.51 us

profile of v6, /device:TPU:1, one launch (start us, length us, event | category | flops | bytes accessed | tf_op | source)
XLA Modules:
  0.0 73.5 jit_solution(4918029779461766116)
XLA Ops:
  0.6 71.3 %ffn_backward.1 = (bf16[32,384]{1,0:T(8,128)(2,1)S(1)}, bf16[384,1536]{1,0:T(8,128)(2,1)S(1)}, bf16[1536,384]{1,0:T(8,128)(2,1)S(1)}) custom-call(bf16[32,384]{1,0:T(8,128)(2,1)} %inputs.1, bf16[32,384]{1,0:T(8,128)(2,1)} %out_grad.1, bf16[384,1536]{1,0:T(8,128)(2,1)} %w_in.1, bf16[1536,384]{1,0:T(8,128)(2,1)} %w_out.1), custom_call_target="tpu_custom_call" | custom-call | flops 6000000000 | bytes 5000000 | tf_op jit(solution)/shard_map/ffn_backward/pallas_call | solution.py:479
  71.9 1.5 %store_results.1 = (bf16[32,384]{1,0:T(8,128)(2,1)}, bf16[384,1536]{1,0:T(8,128)(2,1)}, bf16[1536,384]{1,0:T(8,128)(2,1)}) custom-call(bf16[32,384]{1,0:T(8,128)(2,1)S(1)} %get-tuple-element.6.refs_0_, bf16[384,1536]{1,0:T(8,128)(2,1)S(1)} %get-tuple-element.7.refs_1_, bf16[1536,384]{1,0:T(8,128)(2,1)S(1)} %get-tuple-element.8.refs_2_), custom_call_target="tpu_custom_call" | custom-call | tf_op jit(solution)/shard_map/store_results/pallas_call | solution.py:514
